TPU v7x, 512 devices: a whole 4x8x8 slice. The times are simulated.
512 devices in a mesh: chan: 64 (over x, z_lo, y), tile: 4 (over z_hi), cores: 2 (over core).
Axes of the slice: x: 4, y: 8, z: 8 (z_hi: 4, z_lo: 2; z = z_hi * 2 + z_lo), core: 2. Of those that a mesh axis runs over, the one named last changes fastest.
Arguments:
- samples: bfloat16 [8, 256, 131840], P(('tile', 'cores'), 'chan'), may hold values from -6 to 6
- filter_taps: float32 [4, 256], replicated, may hold values from -3 to 3
- kept_channels: int32 [64], replicated, may hold values from 0 to 255
- input_flags: int32 [8, 256], P(('tile', 'cores'), 'chan'), may hold values 0 or 1
Outputs:
- visibilities: float32 [64, 2, 2048, 2048], P('chan', None, ('tile', 'cores'))
All inputs are finite; a program needn't handle non-finite values. No bound on the sum of `input_flags` on one device may be relied on, other than what follows from the above.
Results may differ from a plain program's by a relative error of at most 0.0035.
Values may be sent and summed in bfloat16 or wider, within the bound.
A program may use at most 64 MiB of HBM per device.

v0:
```python
import math

import jax
import jax.numpy as jnp
from jax import lax
from jax.sharding import PartitionSpec as P


def dft_table(kept_channels, points):
    index = jnp.arange(points, dtype=jnp.int32)
    product = kept_channels[:, None] * index[None, :] % points
    phase = product.astype(jnp.float32) * (2.0 * math.pi / points)
    scaled = 1.0 / math.sqrt(points)
    table = jnp.stack([jnp.cos(phase) * scaled, -jnp.sin(phase) * scaled], axis=1)
    return table.reshape(2 * kept_channels.shape[0], points)


def make_correlate(own, spectra, piece):
    row_count = own.shape[1]
    left = jnp.concatenate(
        [jnp.concatenate([own[0], own[1]], axis=1), jnp.concatenate([own[1], -own[0]], axis=1)],
        axis=0,
    )
    right = jnp.concatenate([piece[0], piece[1]], axis=1)
    block = lax.dot_general(
        left, right, (((1,), (1,)), ((), ())), preferred_element_type=jnp.float32
    )
    return (block * (1.0 / spectra)).reshape(1, 2, row_count, piece.shape[1])


def per_device(samples, filter_taps, kept_channels, input_flags):
    taps, points = filter_taps.shape
    local_inputs = samples.shape[1]
    frame_count = samples.shape[2] // points
    spectra = frame_count - taps + 1
    frames = samples[0].reshape(local_inputs, frame_count, points)
    filtered = filter_taps[0][None, None, :] * frames[:, 0:spectra, :].astype(jnp.float32)
    for step in range(1, taps):
        filtered = filtered + filter_taps[step][None, None, :] * frames[
            :, step : step + spectra, :
        ].astype(jnp.float32)
    table = dft_table(kept_channels, points)
    spectrum = jnp.einsum("rp,isp->ris", table, filtered, precision=lax.Precision.HIGHEST)
    spectrum = spectrum * input_flags[0].astype(jnp.float32)[None, :, None]
    channels = kept_channels.shape[0]
    spectrum = spectrum.astype(jnp.bfloat16).reshape(channels, 2, 1, local_inputs, spectra)
    group_inputs = local_inputs * lax.axis_size("chan")
    turned = lax.all_to_all(spectrum, "chan", split_axis=0, concat_axis=3, tiled=True)
    own = turned.reshape(2, group_inputs, spectra)
    result = make_correlate(
        own, spectra, lax.all_gather(own, ("tile", "cores"), axis=1, tiled=True)
    )
    return result


def solution(mesh):
    in_specs = (P(("tile", "cores"), "chan", None), P(), P(), P(("tile", "cores"), "chan"))
    out_specs = P("chan", None, ("tile", "cores"), None)
    return jax.shard_map(
        per_device, mesh=mesh, in_specs=in_specs, out_specs=out_specs, check_vma=False
    )
```

profile of v0, /device:TPU:1, one launch (start us, length us, event | category | flops | bytes accessed | tf_op | source)
XLA Modules:
  0.0 122.3 jit_solution(6685828086408246060)
XLA Ops:
  6.5 0.0 copy-start
  6.5 0.0 all-gather.2.cloned.1.call-start
  6.5 0.8 fusion.48
  7.4 1.0 cosine_multiply_fusion
  8.4 0.1 copy.15
  8.5 0.1 reshape.131
  8.6 1.9 %reshape_squeeze.3 = bf16[4,515,256]{2,1,0:T(8,128)(2,1)S(1)} reshape(bf16[1,4,131840]{2,1,0:T(4,128)(2,1)} %param.4) | data formatting | bytes 2109440 | tf_op jit(solution)/shard_map/reshape;squeeze | solution.py:36
  10.5 0.0 copy-done
  10.5 3.0 %fusion.22 = bf16[128,4,512]{2,0,1:T(8,128)(2,1)S(1)} fusion(f32[128,256,1]{1,0,2:T(8,128)S(1)} %reshape.131, bf16[4,515,256]{2,1,0:T(8,128)(2,1)S(1)} %reshape_squeeze.3, f32[256]{0:T(256)S(1)} %bitcast.23, f32[256]{0:T(256)S(1)} %bitcast.24, f32[256]{0:T(256)S(1)} %bitcast.22, f32[256]{0:T(256)S(1)} %bitcast.21, f32[4]{0:T(128)S(1)} %convert_bitcast_fusion), kind=kOutput, calls=%fused_computation.20 | convolution fusion | flops 811597824 | bytes 4854272 | tf_op jit(solution)/shard_map/rp,isp->ris/dot_general | solution.py:43
  13.5 0.2 reshape.128
  13.8 0.4 copy.16
  14.1 28.7 %all_to_all.15 = bf16[64,2,1,4,512]{4,1,3,2,0:T(2,128)(2,1)} all-to-all(bf16[64,2,1,4,512]{4,1,3,2,0:T(2,128)(2,1)S(1)} %copy.16), channel_id=1, replica_groups=mesh['chan'=64,'tile'=4,'cores'=2] {'chan'}, dimensions={0} | all-to-all | bytes 1048576 | tf_op jit(solution)/shard_map/all_to_all | solution.py:48
  42.9 0.0 all-gather.2.cloned.1.call-update
  42.9 3.7 %slice_reduce_fusion = (bf16[64,4,512]{2,1,0:T(4,128)(2,1)S(1)}, bf16[64,4,512]{2,1,0:T(4,128)(2,1)S(1)}) fusion(bf16[1,2,1,64,4,512]{5,1,4,3,2,0:T(2,128)(2,1)} %bitcast.20), kind=kLoop, calls=%fused_computation.36 | loop fusion | bytes 1048576 | tf_op jit(solution)/shard_map/slice | solution.py:21
  46.6 0.1 squeeze.15
  46.7 0.1 squeeze.16
  46.8 54.1 %all-gather.2.cloned.1.call-done = bf16[2,2048,512]{2,0,1:T(2,128)(2,1)} async-done(((bf16[2,256,512]{2,0,1:T(2,128)(2,1)}), bf16[2,2048,512]{2,0,1:T(2,128)(2,1)}) %all-gather.2.cloned.1.call-update) | async-done | bytes 4194320 | tf_op jit(solution)/shard_map/all_gather | solution.py:51
  100.9 9.0 %fusion.47 = (bf16[1,2048,512]{2,0,1:T(2,128)(2,1)S(1)}, bf16[1,2048,512]{2,0,1:T(2,128)(2,1)S(1)}) fusion(bf16[2,2048,512]{2,0,1:T(2,128)(2,1)} %all-gather.2.cloned.1.call-done), kind=kLoop, calls=%fused_computation.52 | loop fusion | bytes 8388608 | tf_op jit(solution)/shard_map/slice | solution.py:24
  109.9 1.2 %copy_bitcast_fusion = (bf16[2048,512]{1,0:T(8,128)(2,1)S(1)}, bf16[2048,512]{1,0:T(8,128)(2,1)S(1)}) fusion(bf16[1,2048,512]{2,0,1:T(2,128)(2,1)S(1)} %get-tuple-element.8, bf16[1,2048,512]{2,0,1:T(2,128)(2,1)S(1)} %get-tuple-element.7), kind=kLoop, calls=%fused_computation.5 | loop fusion | bytes 8388608 | tf_op jit(solution)/shard_map/squeeze | solution.py:24
  111.1 4.4 %fusion.4 = f32[512,2048]{1,0:T(8,128)} fusion(bf16[2048,512]{1,0:T(8,128)(2,1)S(1)} %get-tuple-element.15, bf16[2048,512]{1,0:T(8,128)(2,1)S(1)} %get-tuple-element.16, bf16[256,512]{1,0:T(8,128)(2,1)S(1)} %neg.14, bf16[256,512]{1,0:T(8,128)(2,1)S(1)} %squeeze.16, bf16[256,512]{1,0:T(8,128)(2,1)S(1)} %squeeze.15), kind=kOutput, calls=%fused_computation.4 | convolution fusion | flops 2161115136 | bytes 9175040 | tf_op jit(solution)/shard_map/dot_general | solution.py:25
  (3 shorter events, 0.1 us)
Async XLA Ops:
  6.5 3.9 %copy-start = (s32[1,4]{1,0:T(1,128)S(1)}, s32[1,4]{1,0:T(1,128)}, u32[]{:S(2)}) copy-start(s32[1,4]{1,0:T(1,128)} %param.7) | copy-start | bytes 52
  6.5 94.3 %all-gather.2.cloned.1.call-start = ((), (), s32[]{:S(2)}) async-start(), calls=%async_computation.1 | async-start | bytes 4718592 | tf_op jit(solution)/shard_map/all_gather | solution.py:51
Sparse Core Ops, SparseCore 0:
  43.0 57.8 all-gather.1
where the time goes:
time: 123 us; the launch traced here: 122 us
  waiting for transfers between devices  54.1 us (44%)
  blocking collectives  28.7 us (23%)
  local copies, waits for them, and re-layouts  17.5 us (14%)
  between operations  13.5 us (11%)
  matrix products  7.42 us (6%)
    all_gather x1, waiting for transfers between devices, per_device(): lax.all_gather(own, ('tile', 'cores'), axis=1, tiled=True)  54.1 us
    all_to_all x1, blocking collectives, per_device(): lax.all_to_all(spectrum, 'chan', split_axis=0, concat_axis=3, tiled=True)  28.7 us
    slice x1, local copies, waits for them, and re-layouts, make_correlate(): right = jnp.concatenate([piece[0], piece[1]], axis=1)  8.99 us
    dot_general x1, matrix products, make_correlate(): lax.dot_general(left, right, (((1,), (1,)), ((), ())), preferred_element_...  4.38 us
    slice x1, local copies, waits for them, and re-layouts, make_correlate(): own[1]  3.68 us
    dot_general x1, matrix products, per_device(): jnp.einsum('rp,isp->ris', table, filtered, precision=lax.Precision.HIGHEST)  3.04 us
  transfers between devices with their start and end apart: 1, of which 1 were waited for; matrix products, arithmetic and copies ran while one was open for 3% of the time, Pallas kernels for 0%

commit v1 on v0

v1 whole, which is shorter than its diff:
```python
import functools
import math

import jax
import jax.numpy as jnp
import numpy as np
from jax import lax
from jax.experimental import pallas as pl
from jax.experimental.pallas import tpu as pltpu
from jax.sharding import PartitionSpec as P

MESH = pl.DeviceIdType.MESH
F32, BF16 = jnp.float32, jnp.bfloat16
NX, NY, NZ = 4, 8, 8
CH = 4
NT = (((1,), (1,)), ((), ()))


def place():
    chan, tile, core = lax.axis_index("chan"), lax.axis_index("tile"), lax.axis_index("cores")
    return chan // (2 * NY), chan % NY, tile * 2 + (chan // NY) % 2, core


def device(x, y, z, core):
    x, y, z = x % NX, y % NY, z % NZ
    return ((x * 2 + z % 2) * NY + y, z // 2, core)


def twiddles(points):
    phase = (np.outer(np.arange(points), np.arange(points)) % points) * (2.0 * math.pi / points)
    whole = np.concatenate([np.cos(phase), -np.sin(phase)], axis=1) / math.sqrt(points)
    whole = whole.astype(np.float32)
    high = whole.astype(BF16)
    low = (whole - high.astype(np.float32)).astype(BF16)
    return np.stack([high, low])


def channel_rows():
    rows = np.zeros((2 * NX * 2 * NY, NX * 2 * NY), np.float32)
    for yc in range(NY):
        for xc in range(NX):
            for zl in range(2):
                for q in range(2):
                    rows[((yc * NX + xc) * 2 + zl) * 2 + q, (xc * 2 + zl) * NY + yc] = 1.0
    return rows.astype(BF16)


def spectra_kernel(samples, taps, kept, flags, twiddle, select, out, table, wide):
    points = taps.shape[1]
    blocks = samples.shape[2] // 128
    inputs = samples.shape[1]
    chosen = (lax.broadcasted_iota(jnp.int32, (points, kept.shape[1]), 0) == kept[...]).astype(F32).astype(BF16)
    onehot = lax.dot_general(select[...], chosen, NT, preferred_element_type=F32).astype(BF16)
    odd = lax.broadcasted_iota(jnp.int32, (onehot.shape[0], points), 0) % 2 == 1
    for part in range(2):
        both = jnp.dot(onehot, twiddle[part], preferred_element_type=F32)
        table[part] = jnp.where(odd, both[:, points:], both[:, :points]).astype(BF16)

    unroll = 10

    def widen(step, _):
        for u in range(unroll):
            block = step * unroll + u
            piece = samples[0, :, pl.ds(pl.multiple_of(block * 128, 128), 128)].astype(F32)
            wide[pl.ds(pl.multiple_of(block * inputs, inputs), inputs), :] = piece
        return 0

    lax.fori_loop(0, blocks // unroll, widen, 0)
    stride = 2 * inputs

    def chunk(h, _):
        for i in range(inputs):
            halves = []
            for half in range(2):
                total = None
                for t in range(taps.shape[0]):
                    rows = wide[pl.ds((h * 128 + t) * stride + half * inputs + i, 128, stride=stride), :]
                    term = taps[pl.ds(t, 1), pl.ds(half * 128, 128)] * rows
                    total = term if total is None else total + term
                halves.append(total)
            filtered = jnp.concatenate(halves, axis=1)
            high = filtered.astype(BF16)
            low = (filtered - high.astype(F32)).astype(BF16)
            spectrum = lax.dot_general(table[0], high, NT, preferred_element_type=F32)
            spectrum += lax.dot_general(table[0], low, NT, preferred_element_type=F32)
            spectrum += lax.dot_general(table[1], high, NT, preferred_element_type=F32)
            spectrum = spectrum * flags[0, i].astype(F32)
            out[h, :, i] = spectrum.astype(BF16).reshape(out.shape[1], out.shape[3], 128)
        return 0

    lax.fori_loop(0, CH, chunk, 0)


def turn_kernel(spec, out, yr, wide, xs, held, ysend, yrecv, xsend, xrecv, zsend, zrecv, csend, crecv, own):
    x, y, z, k = place()
    sib = device(x, y, z, 1 - k)
    barrier = pltpu.get_barrier_semaphore()
    partners = [device(x, y + d, z, k) for d in range(1, NY)]
    partners += [device(x + d, y, z, k) for d in range(1, NX)]
    partners += [device(x, y, z + d, k) for d in (1, 2, NZ - 1, NZ - 2)] + [sib]
    for d in partners:
        pl.semaphore_signal(barrier, inc=1, device_id=d, device_id_type=MESH)
    pl.semaphore_wait(barrier, len(partners))

    def remote(src, dst, ssem, rsem, dev):
        pltpu.make_async_remote_copy(
            src_ref=src, dst_ref=dst, send_sem=ssem, recv_sem=rsem, device_id=dev, device_id_type=MESH
        ).start()

    def wait(ref, sem):
        pltpu.make_async_copy(ref, ref, sem).wait()

    def slot(h, d):
        src = (z + d) % NZ
        return out.at[h, (src // 2) * 2 + k, src % 2]

    def send_y(h):
        pltpu.make_async_copy(spec.at[h, y], yr.at[h, y], yrecv.at[h]).start()
        for d in (4, 3, 5, 2, 6, 1, 7):
            to = (y + d) % NY
            remote(spec.at[h, to], yr.at[h, y], ysend, yrecv.at[h], device(x, y + d, z, k))

    def turn(h):
        wide[...] = yr[h].reshape(wide.shape).astype(F32)
        for r in range(16):
            rows = wide[pl.ds(r, 32, stride=16), :]
            xs[h, r // 4, (r // 2) % 2, r % 2] = rows.astype(BF16)

    def send_x(h):
        pltpu.make_async_copy(xs.at[h, x], held.at[h, x], xrecv.at[h]).start()
        for d in (2, 1, 3):
            to = (x + d) % NX
            remote(xs.at[h, to], held.at[h, x], xsend, xrecv.at[h], device(x + d, y, z, k))

    def forward(h, d):
        remote(slot(h, d), slot(h, d), csend, crecv, sib)

    def send_z(h):
        same, other = held.at[h, :, z % 2], held.at[h, :, 1 - z % 2]
        remote(same, slot(h, 0), zsend, zrecv.at[h, 2], device(x, y, z + 2, k))
        remote(same, slot(h, 0), zsend, zrecv.at[h, 3], device(x, y, z - 2, k))
        remote(other, slot(h, 0), zsend, zrecv.at[h, 0], device(x, y, z + 1, k))
        remote(other, slot(h, 0), zsend, zrecv.at[h, 1], device(x, y, z - 1, k))
        pltpu.make_async_copy(same, slot(h, 0), own).start()
        remote(same, slot(h, 0), csend, crecv, sib)

    def relay_z(h):
        sign = 1 - 2 * ((h + k) % 2)
        wait(slot(h, -1), zrecv.at[h, 0])
        remote(slot(h, -1), slot(h, -1), zsend, zrecv.at[h, 4], device(x, y, z + 2, k))
        wait(slot(h, 1), zrecv.at[h, 1])
        remote(slot(h, 1), slot(h, 1), zsend, zrecv.at[h, 5], device(x, y, z - 2, k))
        wait(slot(h, -2), zrecv.at[h, 2])
        wait(slot(h, 2), zrecv.at[h, 3])
        remote(slot(h, -2 * sign), slot(h, -2 * sign), zsend, zrecv.at[h, 6], device(x, y, z + 2 * sign, k))
        for d in (-1, 1, -2, 2):
            forward(h, d)

    def finish_z(h):
        wait(slot(h, -3), zrecv.at[h, 4])
        forward(h, -3)
        wait(slot(h, 3), zrecv.at[h, 5])
        forward(h, 3)
        wait(slot(h, 4), zrecv.at[h, 6])
        forward(h, 4)

    send_y(0)
    for h in range(CH):
        wait(yr.at[h], yrecv.at[h])
        if h + 1 < CH:
            send_y(h + 1)
        turn(h)
        send_x(h)
        wait(held.at[h], xrecv.at[h])
        send_z(h)
        if h >= 1:
            relay_z(h - 1)
        if h >= 2:
            finish_z(h - 2)
    relay_z(CH - 1)
    finish_z(CH - 2)
    finish_z(CH - 1)

    wait(out.at[:, pl.ds(0, 4)], crecv)
    wait(out.at[:, pl.ds(0, 4)], csend)
    wait(spec.at[:, pl.ds(0, NY - 1)], ysend)
    wait(xs.at[:, pl.ds(0, NX - 1)], xsend)
    wait(out.at[:, pl.ds(0, 7), 0], zsend)
    wait(out.at[:, 0, 0], own)


def correlate_kernel(scale, spectra, own_hbm, out, own, left, right, sem):
    step = pl.program_id(0)
    rows = out.shape[2]

    def lay(block, h, q):
        pieces = [block[h, zl, xx, q] for xx in range(NX) for zl in range(2)]
        return jnp.concatenate(pieces, axis=0)

    @pl.when(step == 0)
    def _():
        mine = lax.axis_index("tile") * 2 + lax.axis_index("cores")
        copy = pltpu.make_async_copy(own_hbm.at[:, mine], own, sem)
        copy.start()
        copy.wait()
        for h in range(CH):
            for q in range(2):
                block = lay(own, h, q)
                left[pl.ds(0, rows), pl.ds((h * 2 + q) * 128, 128)] = block
                left[pl.ds(rows, rows), pl.ds((h * 2 + 1 - q) * 128, 128)] = block if q else -block

    for h in range(CH):
        for q in range(2):
            right[:, pl.ds((h * 2 + q) * 128, 128)] = lay(spectra.at[:, 0], h, q)
    block = lax.dot_general(left[...], right[...], NT, preferred_element_type=F32) * scale
    out[0] = block.reshape(2, rows, block.shape[1])


def per_device(samples, filter_taps, kept_channels, input_flags):
    taps, points = filter_taps.shape
    inputs, length = samples.shape[1:]
    frames = length // points
    count = frames - taps + 1
    channels = kept_channels.shape[0]
    vmem, hbm = pl.BlockSpec(memory_space=pltpu.VMEM), pl.BlockSpec(memory_space=pl.ANY)
    dma = pltpu.SemaphoreType.DMA

    spec = pl.pallas_call(
        spectra_kernel,
        out_shape=jax.ShapeDtypeStruct((CH, NY, inputs, 2 * channels // NY, 128), BF16),
        in_specs=[vmem, vmem, vmem, pl.BlockSpec(memory_space=pltpu.SMEM), vmem, vmem],
        out_specs=vmem,
        scratch_shapes=[
            pltpu.VMEM((2, 2 * channels, points), BF16),
            pltpu.VMEM((length // 128 * inputs, 128), F32),
        ],
        compiler_params=pltpu.CompilerParams(vmem_limit_bytes=32 << 20),
        name="spectra",
    )(
        samples,
        filter_taps,
        kept_channels.reshape(1, channels),
        input_flags,
        jnp.asarray(twiddles(points)),
        jnp.asarray(channel_rows()),
    )

    gathered = pl.pallas_call(
        turn_kernel,
        out_shape=jax.ShapeDtypeStruct((CH, 8, 2, NX, 2, 32, 128), BF16),
        in_specs=[hbm],
        out_specs=hbm,
        scratch_shapes=[
            pltpu.VMEM((CH, NY, inputs, 16, 128), BF16),
            pltpu.VMEM((NY * inputs * 16, 128), F32),
            pltpu.VMEM((CH, NX, 2, 2, 32, 128), BF16),
            pltpu.VMEM((CH, NX, 2, 2, 32, 128), BF16),
            dma,
            dma((CH,)),
            dma,
            dma((CH,)),
            dma,
            dma((CH, 7)),
            dma,
            dma,
            dma,
        ],
        compiler_params=pltpu.CompilerParams(
            collective_id=0, has_side_effects=True, vmem_limit_bytes=32 << 20
        ),
        name="turn",
    )(spec)

    rows = 256
    return pl.pallas_call(
        functools.partial(correlate_kernel, 1.0 / count),
        grid=(8,),
        out_shape=jax.ShapeDtypeStruct((1, 2, rows, 8 * rows), F32),
        in_specs=[pl.BlockSpec((CH, 1, 2, NX, 2, 32, 128), lambda b: (0, b, 0, 0, 0, 0, 0)), hbm],
        out_specs=pl.BlockSpec((1, 2, rows, rows), lambda b: (0, 0, 0, b)),
        scratch_shapes=[
            pltpu.VMEM((CH, 2, NX, 2, 32, 128), BF16),
            pltpu.VMEM((2 * rows, 2 * count), BF16),
            pltpu.VMEM((rows, 2 * count), BF16),
            dma,
        ],
        compiler_params=pltpu.CompilerParams(vmem_limit_bytes=32 << 20),
        name="correlate",
    )(gathered, gathered)


def solution(mesh):
    in_specs = (P(("tile", "cores"), "chan", None), P(), P(), P(("tile", "cores"), "chan"))
    out_specs = P("chan", None, ("tile", "cores"), None)
    return jax.shard_map(
        per_device, mesh=mesh, in_specs=in_specs, out_specs=out_specs, check_vma=False
    )
```

time: 123 us -> 78 us (0.63)
  Pallas kernels: 0 us -> 72.6 us
  waiting for transfers between devices: 54.1 us -> 0 us
  blocking collectives: 28.7 us -> 0 us
  between operations: 13.5 us -> 0.02 us
  local copies, waits for them, and re-layouts: 17.5 us -> 5.02 us
  matrix products: 7.42 us -> 0 us
    pallas_call x0 -> x3, Pallas kernels: none -> 72.6 us  [the longest x1 61.5 us: per_device(): pl.pallas_call(turn_kernel, out_shape=jax.ShapeDtypeStruct((CH, 8, 2, NX,...]
    all_gather x1 -> x0, waiting for transfers between devices: 54.1 us -> none  [per_device(): lax.all_gather(own, ('tile', 'cores'), axis=1, tiled=True)]
    all_to_all x1 -> x0, blocking collectives: 28.7 us -> none  [per_device(): lax.all_to_all(spectrum, 'chan', split_axis=0, concat_axis=3, tiled=True)]
    slice x3 -> x0, local copies, waits for them, and re-layouts: 13.5 us -> none  [the longest x1 8.99 us: make_correlate(): right = jnp.concatenate([piece[0], piece[1]], axis=1)]
    dot_general x2 -> x0, matrix products: 7.42 us -> none  [the longest x1 4.38 us: make_correlate(): lax.dot_general(left, right, (((1,), (1,)), ((), ())), preferred_element_...]
    unnamed x2 -> x12, local copies, waits for them, and re-layouts: 0.01 us -> 5.02 us
    another operation x2 -> x0, local copies, waits for them, and re-layouts: 1.97 us -> none  [the longest x1 1.87 us: per_device(): frames = samples[0].reshape(local_inputs, frame_count, points)]
    squeeze x3 -> x0, local copies, waits for them, and re-layouts: 1.37 us -> none  [the longest x1 1.24 us: make_correlate(): right = jnp.concatenate([piece[0], piece[1]], axis=1)]
  transfers between devices with their start and end apart: 1 -> 0, of which waited for: 1 -> 0; matrix products, arithmetic and copies ran while one was open for 3% -> 0% of each run, Pallas kernels for 0% -> 0%
where the time goes in v1:
time: 78 us; the launch traced here: 77.7 us
  Pallas kernels  72.6 us (93%)
  local copies, waits for them, and re-layouts  5.02 us (6%)
    pallas_call x1, Pallas kernels, per_device(): pl.pallas_call(turn_kernel, out_shape=jax.ShapeDtypeStruct((CH, 8, 2, NX,...  61.5 us
    pallas_call x1, Pallas kernels, per_device(): pl.pallas_call(functools.partial(correlate_kernel, 1.0 / count), grid=(8,...  6.22 us
    unnamed x12, local copies, waits for them, and re-layouts  5.02 us
    pallas_call x1, Pallas kernels, per_device(): pl.pallas_call(spectra_kernel, out_shape=jax.ShapeDtypeStruct((CH, NY, in...  4.93 us

profile of v1, /device:TPU:1, one launch (start us, length us, event | category | flops | bytes accessed | tf_op | source)
XLA Modules:
  0.0 77.7 jit_solution(16158159792979495131)
XLA Ops:
  0.0 0.0 copy-start
  0.0 1.2 %copy-done = bf16[1,4,131840]{2,1,0:T(4,128)(2,1)S(1)} copy-done((bf16[1,4,131840]{2,1,0:T(4,128)(2,1)S(1)}, bf16[1,4,131840]{2,1,0:T(4,128)(2,1)}, u32[]{:S(2)}) %copy-start) | copy-done | bytes 1054744
  1.2 0.0 copy-start.1
  1.2 1.0 %copy-done.1 = bf16[2,256,512]{2,1,0:T(8,128)(2,1)S(1)} copy-done((bf16[2,256,512]{2,1,0:T(8,128)(2,1)S(1)}, bf16[2,256,512]{2,1,0:T(8,128)(2,1)}, u32[]{:S(2)}) %copy-start.1) | copy-done | bytes 524312
  2.3 0.0 copy-start.2
  2.3 0.8 copy-done.2
  3.0 0.0 copy-start.3
  3.0 0.7 copy-done.3
  3.7 0.0 copy-start.4
  3.7 0.7 copy-done.4
  4.4 0.0 copy-start.5
  4.4 0.7 copy-done.5
  5.0 4.9 %spectra.1.spec = bf16[4,8,4,16,128]{4,3,2,1,0:T(8,128)(2,1)S(1)} custom-call(bf16[1,4,131840]{2,1,0:T(4,128)(2,1)S(1)} %copy-done, f32[4,256]{1,0:T(4,128)S(1)} %copy-done.3, s32[1,64]{1,0:T(1,128)S(1)} %bitcast.1, s32[1,4]{1,0:T(1,128)S(1)} %copy-done.5, bf16[2,256,512]{2,1,0:T(8,128)(2,1)S(1)} %copy-done.1, bf16[128,64]{1,0:T(8,128)(2,1)S(1)} %copy-done.2), custom_call_target="tpu_custom_call" | custom-call | tf_op jit(solution)/shard_map/spectra/pallas_call | solution.py:228
  10.0 61.5 %turn.1.spectra.own_hbm = bf16[4,8,2,4,2,32,128]{6,5,4,3,2,1,0:T(8,128)(2,1)S(1)} custom-call(bf16[4,8,4,16,128]{4,3,2,1,0:T(8,128)(2,1)S(1)} %spectra.1.spec), custom_call_target="tpu_custom_call" | custom-call | tf_op jit(solution)/shard_map/turn/pallas_call | solution.py:248
  71.5 6.2 %correlate.1 = f32[1,2,256,2048]{3,2,1,0:T(8,128)} custom-call(bf16[4,8,2,4,2,32,128]{6,5,4,3,2,1,0:T(8,128)(2,1)S(1)} %turn.1.spectra.own_hbm, bf16[4,8,2,4,2,32,128]{6,5,4,3,2,1,0:T(8,128)(2,1)S(1)} %turn.1.spectra.own_hbm), custom_call_target="tpu_custom_call" | custom-call | tf_op jit(solution)/shard_map/correlate/pallas_call | solution.py:275
Async XLA Ops:
  0.0 1.2 %copy-start = (bf16[1,4,131840]{2,1,0:T(4,128)(2,1)S(1)}, bf16[1,4,131840]{2,1,0:T(4,128)(2,1)}, u32[]{:S(2)}) copy-start(bf16[1,4,131840]{2,1,0:T(4,128)(2,1)} %samples.1) | copy-start | bytes 3164164
  1.2 1.0 %copy-start.1 = (bf16[2,256,512]{2,1,0:T(8,128)(2,1)S(1)}, bf16[2,256,512]{2,1,0:T(8,128)(2,1)}, u32[]{:S(2)}) copy-start(bf16[2,256,512]{2,1,0:T(8,128)(2,1)} %constant.4.clone.twiddle) | copy-start | bytes 1572868
  2.3 0.8 copy-start.2
  3.0 0.7 copy-start.3
  3.7 0.7 copy-start.4
  4.4 0.7 copy-start.5

commit v2 on v0

v2 whole, which is shorter than its diff:
```python
import functools
import math

import jax
import jax.numpy as jnp
import numpy as np
from jax import lax
from jax.experimental import pallas as pl
from jax.experimental.pallas import tpu as pltpu
from jax.sharding import PartitionSpec as P

MESH = pl.DeviceIdType.MESH
F32, BF16 = jnp.float32, jnp.bfloat16
NX, NY, NZ = 4, 8, 8
CH = 4
NT = (((1,), (1,)), ((), ()))
REL = (0, -1, 1, -2, 2, -3, 3, 4)


def place():
    chan, tile, core = lax.axis_index("chan"), lax.axis_index("tile"), lax.axis_index("cores")
    return chan // (2 * NY), chan % NY, tile * 2 + (chan // NY) % 2, core


def device(x, y, z, core):
    x, y, z = x % NX, y % NY, z % NZ
    return ((x * 2 + z % 2) * NY + y, z // 2, core)


def twiddles(points):
    phase = (np.outer(np.arange(points), np.arange(points)) % points) * (2.0 * math.pi / points)
    whole = np.concatenate([np.cos(phase), -np.sin(phase)], axis=1) / math.sqrt(points)
    whole = whole.astype(np.float32)
    high = whole.astype(BF16)
    low = (whole - high.astype(np.float32)).astype(BF16)
    return np.stack([high, low])


def body(
    scale, samples_hbm, taps_hbm, kept_hbm, flags_hbm, twiddle_hbm, vis,
    samples, taps, kept, flags, twiddle, table, wide, first, spec, yr, turned, xs, held, za, zb, zx, got, left,
    load, ysend, yrecv, xsend, xrecv, zsend, zrecv, csend, crecv, own, y0send, y0recv, x0send, x0recv,
):
    x, y, z, k = place()
    points = taps.shape[1]
    inputs = samples.shape[1]
    chunk_blocks, extra = 256, 2 * (taps.shape[0] - 1)

    def wait(ref, sem):
        pltpu.make_async_copy(ref, ref, sem).wait()

    def remote(src, dst, ssem, rsem, dev):
        pltpu.make_async_remote_copy(
            src_ref=src, dst_ref=dst, send_sem=ssem, recv_sem=rsem, device_id=dev, device_id_type=MESH
        ).start()

    def part(h):
        start = 0 if h == 0 else h * chunk_blocks + extra
        size = chunk_blocks + (extra if h == 0 else 0)
        return start, size

    def piece(h):
        start, size = part(h)
        return pl.ds(start * 128, size * 128)

    small = [(kept_hbm, kept), (twiddle_hbm, twiddle), (taps_hbm, taps), (flags_hbm, flags)]
    loads = [pltpu.make_async_copy(src, dst, load.at[CH + n]) for n, (src, dst) in enumerate(small)]
    for h in range(CH):
        loads.append(
            pltpu.make_async_copy(samples_hbm.at[:, :, piece(h)], samples.at[:, :, piece(h)], load.at[h])
        )
    for copy in loads:
        copy.start()

    sib = device(x, y, z, 1 - k)
    barrier = pltpu.get_barrier_semaphore()
    partners = [device(x, y + d, z, k) for d in range(1, NY)]
    partners += [device(x + d, y, z, k) for d in range(1, NX)]
    partners += [device(x, y, z + d, k) for d in (1, 2, NZ - 1, NZ - 2)] + [sib]
    for d in partners:
        pl.semaphore_signal(barrier, inc=1, device_id=d, device_id_type=MESH)

    for copy in loads[:4]:
        copy.wait()
    chosen = (lax.broadcasted_iota(jnp.int32, (points, kept.shape[1]), 0) == kept[...]).astype(F32).astype(BF16)
    row = lax.broadcasted_iota(jnp.int32, (table.shape[2], kept.shape[1]), 0)
    column = lax.broadcasted_iota(jnp.int32, row.shape, 1)
    orders = (
        (((row >> 1) & 3) * 2 + (row >> 6)) * NY + ((row >> 3) & 7),
        ((row >> 1) & 7) * NY + (row >> 4),
    )
    odd = lax.broadcasted_iota(jnp.int32, (table.shape[2], points), 0) % 2 == 1
    for n, order in enumerate(orders):
        select = (order == column).astype(F32).astype(BF16)
        onehot = lax.dot_general(select, chosen, NT, preferred_element_type=F32).astype(BF16)
        for p in range(2):
            both = jnp.dot(onehot, twiddle[p], preferred_element_type=F32)
            table[n, p] = jnp.where(odd, both[:, points:], both[:, :points]).astype(BF16)

    stride = 2 * inputs

    def widen(h):
        loads[4 + h].wait()
        start, size = part(h)
        unroll = 16 if size % 16 == 0 else 2

        def step(s, _):
            for u in range(unroll):
                block = start + s * unroll + u
                values = samples[0, :, pl.ds(pl.multiple_of(block * 128, 128), 128)].astype(F32)
                wide[pl.ds(pl.multiple_of(block * inputs, inputs), inputs), :] = values
            return 0

        lax.fori_loop(0, size // unroll, step, 0)

    def transform(h, i, n):
        halves = []
        for half in range(2):
            total = None
            for t in range(taps.shape[0]):
                rows = wide[pl.ds((h * 128 + t) * stride + half * inputs + i, 128, stride=stride), :]
                term = taps[pl.ds(t, 1), pl.ds(half * 128, 128)] * rows
                total = term if total is None else total + term
            halves.append(total)
        filtered = jnp.concatenate(halves, axis=1)
        high = filtered.astype(BF16)
        low = (filtered - high.astype(F32)).astype(BF16)
        spectrum = lax.dot_general(table[n, 0], high, NT, preferred_element_type=F32)
        spectrum += lax.dot_general(table[n, 0], low, NT, preferred_element_type=F32)
        spectrum += lax.dot_general(table[n, 1], high, NT, preferred_element_type=F32)
        return spectrum * flags[pl.ds(0, 1), pl.ds(i, 1)].astype(F32)

    def spectra_first():
        widen(0)
        for m in range(inputs // 2):
            pair = [transform(0, 2 * m + i, 0).reshape(2, NY, 8, 128) for i in range(2)]
            first[:, :, m] = jnp.concatenate(pair, axis=2).astype(BF16)

    def spectra(h):
        widen(h)
        for i in range(inputs):
            spec[h - 1, :, i] = transform(h, i, 1).astype(BF16).reshape(NY, 16, 128)

    def send_y(h):
        pltpu.make_async_copy(spec.at[h - 1, y], yr.at[h - 1, y], yrecv.at[h - 1]).start()
        for d in (4, 3, 5, 2, 6, 1, 7):
            to = (y + d) % NY
            remote(spec.at[h - 1, to], yr.at[h - 1, y], ysend, yrecv.at[h - 1], device(x, y + d, z, k))

    def turn(h):
        wait(yr.at[h - 1], yrecv.at[h - 1])
        turned[...] = yr[h - 1].reshape(turned.shape).astype(F32)
        for r in range(16):
            rows = turned[pl.ds(r, 32, stride=16), :]
            xs[h - 1, r // 4, (r // 2) % 2, r % 2] = rows.astype(BF16)

    def send_x(h):
        pltpu.make_async_copy(xs.at[h - 1, x], held.at[h - 1, x], xrecv.at[h - 1]).start()
        for d in (2, 1, 3):
            to = (x + d) % NX
            remote(xs.at[h - 1, to], held.at[h - 1, x], xsend, xrecv.at[h - 1], device(x + d, y, z, k))

    def slot(h, n):
        src = (z + REL[n]) % NZ
        return got.at[h, (src // 2) * 2 + k, src % 2]

    def forward(h, n):
        remote(slot(h, n), slot(h, n), csend, crecv.at[h, n // 5], sib)

    def spread(h, same, other, at):
        remote(same, at(0, 3), zsend, zrecv.at[h, 3], device(x, y, z + 2, k))
        remote(same, at(0, 4), zsend, zrecv.at[h, 4], device(x, y, z - 2, k))
        remote(other, at(0, 1), zsend, zrecv.at[h, 1], device(x, y, z + 1, k))
        remote(other, at(0, 2), zsend, zrecv.at[h, 2], device(x, y, z - 1, k))
        pltpu.make_async_copy(same, at(0, 0), own.at[h]).start()

    def relay(h, at):
        sign = (h + k) % 2
        wait(at(1, 1), zrecv.at[h, 1])
        remote(at(1, 1), at(1, 5), zsend, zrecv.at[h, 5], device(x, y, z + 2, k))
        wait(at(2, 2), zrecv.at[h, 2])
        remote(at(2, 2), at(2, 6), zsend, zrecv.at[h, 6], device(x, y, z - 2, k))
        wait(at(3, 3), zrecv.at[h, 3])
        wait(at(4, 4), zrecv.at[h, 4])
        remote(at(3 + sign, 3 + sign), at(3 + sign, 7), zsend, zrecv.at[h, 7], device(x, y, z + 2 - 4 * sign, k))

    def at_first(_, n):
        return za.at[n]

    def at_slot(h):
        def at(n, _):
            if isinstance(n, int):
                return slot(h, n)
            src = (z - 2 + 4 * (n - 3)) % NZ
            return got.at[h, (src // 2) * 2 + k, src % 2]

        return at

    def send_z(h):
        wait(held.at[h - 1], xrecv.at[h - 1])
        same, other = held.at[h - 1, :, z % 2], held.at[h - 1, :, 1 - z % 2]
        spread(h, same, other, at_slot(h))
        remote(same, slot(h, 0), csend, crecv.at[h, 0], sib)

    def relay_z(h):
        relay(h, at_slot(h))
        for n in range(1, 5):
            forward(h, n)

    def finish_z(h):
        for n in range(5, 8):
            wait(slot(h, n), zrecv.at[h, n])
            forward(h, n)

    groups = ((0, 5), (5, 3))

    def send_y0(g):
        begin, size = groups[g]
        mine = pl.ds(begin, size)
        pltpu.make_async_copy(za.at[mine, y], zb.at[y, mine], y0recv.at[g]).start()
        for d in (4, 3, 5, 2, 6, 1, 7):
            to = (y + d) % NY
            remote(za.at[mine, to], zb.at[y, mine], y0send, y0recv.at[g], device(x, y + d, z, k))

    def turn_send_x0(g):
        begin, size = groups[g]
        wait(zb.at[:, pl.ds(begin, size)], y0recv.at[g])
        for n in range(begin, begin + size):
            turned[pl.ds(0, 256), :] = zb[:, n].reshape(256, 128).astype(F32)
            for r in range(8):
                zx[r // 2, n, r % 2] = turned[pl.ds(r, 32, stride=8), :].astype(BF16)
            src = (z + REL[n]) % NZ
            dst = got.at[0, (src // 2) * 2 + k, src % 2, x]
            pltpu.make_async_copy(zx.at[x, n], dst, x0recv.at[n]).start()
            for d in (2, 1, 3):
                remote(zx.at[(x + d) % NX, n], dst, x0send, x0recv.at[n], device(x + d, y, z, k))

    def finish_x0(g):
        begin, size = groups[g]
        for n in range(begin, begin + size):
            wait(slot(0, n), x0recv.at[n])
            forward(0, n)

    rows = vis.shape[2]

    def lay(h, b, q):
        pieces = [got[h, b, zl, xx, q] for xx in range(NX) for zl in range(2)]
        return jnp.concatenate(pieces, axis=0)

    def lay_left(h):
        mine = (z // 2) * 2 + k
        for q in range(2):
            block = lay(h, mine, q)
            left[pl.ds(0, rows), pl.ds(q * 128, 128)] = block
            left[pl.ds(rows, rows), pl.ds((1 - q) * 128, 128)] = block if q else -block

    def multiply(h, b, start, end):
        right = jnp.concatenate([lay(h, b, 0), lay(h, b, 1)], axis=1)
        block = lax.dot_general(left[...], right, NT, preferred_element_type=F32).reshape(2, rows, rows)
        columns = pl.ds(pl.multiple_of(b * rows, rows), rows)
        if not start:
            block = vis[0, :, :, columns] + block
        vis[0, :, :, columns] = block * scale if end else block

    def wait_sibling(h, g):
        begin, size = groups[g]
        wait(got.at[h, pl.ds(begin, size), 0], crecv.at[h, g])

    def correlate(h, start=False):
        if h:
            wait(slot(h, 0), own.at[h])
        wait_sibling(h, 0)
        wait_sibling(h, 1)
        lay_left(h)

        def step(b, _):
            multiply(h, b, start, False)
            return 0

        lax.fori_loop(0, 8, step, 0)

    def correlate_last(h):
        side = 2 * (z % 2) - 1
        tiles = ((z // 2) % 4, (z // 2 + side) % 4, (z // 2 - side) % 4, (z // 2 + 2) % 4)
        wait(slot(h, 0), own.at[h])
        lay_left(h)
        for t in tiles[:2]:
            multiply(h, t * 2 + k, False, True)
        wait_sibling(h, 0)
        for t in tiles[:2]:
            multiply(h, t * 2 + 1 - k, False, True)
        finish_z(h)
        for t in tiles[2:]:
            multiply(h, t * 2 + k, False, True)
        wait_sibling(h, 1)
        for t in tiles[2:]:
            multiply(h, t * 2 + 1 - k, False, True)

    spectra_first()
    pl.semaphore_wait(barrier, len(partners))
    spread(0, first.at[z % 2], first.at[1 - z % 2], at_first)
    spectra(1)
    send_y(1)
    spectra(2)
    spectra(3)
    relay(0, at_first)
    turn(1)
    send_x(1)
    send_y(2)
    wait(za.at[0], own.at[0])
    send_y0(0)
    send_z(1)
    for n in range(5, 8):
        wait(za.at[n], zrecv.at[0, n])
    send_y0(1)
    turn(2)
    send_x(2)
    send_y(3)
    relay_z(1)
    send_z(2)
    turn_send_x0(0)
    turn(3)
    send_x(3)
    finish_z(1)
    send_z(3)
    relay_z(2)
    turn_send_x0(1)
    correlate(1, start=True)
    finish_x0(0)
    finish_z(2)
    relay_z(3)
    finish_x0(1)
    correlate(2)
    correlate(0)
    correlate_last(3)

    wait(got.at[:, pl.ds(0, 4)], csend)
    wait(got.at[:, pl.ds(0, 7), 0], zsend)
    wait(spec.at[:, pl.ds(0, NY - 1)], ysend)
    wait(xs.at[:, pl.ds(0, NX - 1)], xsend)
    wait(za.at[pl.ds(0, NY - 1)], y0send)
    wait(zx.at[pl.ds(0, NX - 1)], x0send)


def per_device(samples, filter_taps, kept_channels, input_flags):
    taps, points = filter_taps.shape
    inputs, length = samples.shape[1:]
    count = length // points - taps + 1
    channels = kept_channels.shape[0]
    vmem, hbm = pl.BlockSpec(memory_space=pltpu.VMEM), pl.BlockSpec(memory_space=pltpu.HBM)
    dma = pltpu.SemaphoreType.DMA
    rows = 256
    late = CH - 1
    operands = (samples, filter_taps, kept_channels.reshape(1, channels), input_flags, jnp.asarray(twiddles(points)))

    return pl.pallas_call(
        functools.partial(body, 1.0 / count),
        out_shape=jax.ShapeDtypeStruct((1, 2, rows, 8 * rows), F32),
        in_specs=[hbm] * 5,
        out_specs=vmem,
        scratch_shapes=[
            *(pltpu.VMEM(a.shape, a.dtype) for a in operands),
            pltpu.VMEM((2, 2, 2 * channels, points), BF16),
            pltpu.VMEM((length // 128 * inputs, 128), F32),
            pltpu.VMEM((2, NY, 2, 16, 128), BF16),
            pltpu.VMEM((late, NY, inputs, 16, 128), BF16),
            pltpu.VMEM((late, NY, inputs, 16, 128), BF16),
            pltpu.VMEM((NY * inputs * 16, 128), F32),
            pltpu.VMEM((late, NX, 2, 2, 32, 128), BF16),
            pltpu.VMEM((late, NX, 2, 2, 32, 128), BF16),
            pltpu.VMEM((8, NY, 2, 16, 128), BF16),
            pltpu.VMEM((NY, 8, 2, 16, 128), BF16),
            pltpu.VMEM((NX, 8, 2, 32, 128), BF16),
            pltpu.VMEM((CH, 8, 2, NX, 2, 32, 128), BF16),
            pltpu.VMEM((2 * rows, 256), BF16),
            dma((CH + 4,)),
            dma,
            dma((late,)),
            dma,
            dma((late,)),
            dma,
            dma((CH, 8)),
            dma,
            dma((CH, 2)),
            dma((CH,)),
            dma,
            dma((2,)),
            dma,
            dma((8,)),
        ],
        compiler_params=pltpu.CompilerParams(
            collective_id=0, has_side_effects=True, vmem_limit_bytes=40 << 20
        ),
        name="correlator",
    )(*operands)


def solution(mesh):
    in_specs = (P(("tile", "cores"), "chan", None), P(), P(), P(("tile", "cores"), "chan"))
    out_specs = P("chan", None, ("tile", "cores"), None)
    return jax.shard_map(
        per_device, mesh=mesh, in_specs=in_specs, out_specs=out_specs, check_vma=False
    )
```

time: 123 us -> 71.4 us (0.58)
  Pallas kernels: 0 us -> 64.9 us
  waiting for transfers between devices: 54.1 us -> 0 us
  blocking collectives: 28.7 us -> 0 us
  between operations: 13.5 us -> 0.01 us
  local copies, waits for them, and re-layouts: 17.5 us -> 6.28 us
  matrix products: 7.42 us -> 0 us
    pallas_call x0 -> x1, Pallas kernels: none -> 64.9 us  [per_device(): pl.pallas_call(functools.partial(body, 1.0 / count), out_shape=jax.ShapeD...]
    all_gather x1 -> x0, waiting for transfers between devices: 54.1 us -> none  [per_device(): lax.all_gather(own, ('tile', 'cores'), axis=1, tiled=True)]
    all_to_all x1 -> x0, blocking collectives: 28.7 us -> none  [per_device(): lax.all_to_all(spectrum, 'chan', split_axis=0, concat_axis=3, tiled=True)]
    slice x3 -> x0, local copies, waits for them, and re-layouts: 13.5 us -> none  [the longest x1 8.99 us: make_correlate(): right = jnp.concatenate([piece[0], piece[1]], axis=1)]
    dot_general x2 -> x0, matrix products: 7.42 us -> none  [the longest x1 4.38 us: make_correlate(): lax.dot_general(left, right, (((1,), (1,)), ((), ())), preferred_element_...]
    unnamed x2 -> x11, local copies, waits for them, and re-layouts: 0.01 us -> 6.28 us
    another operation x2 -> x0, local copies, waits for them, and re-layouts: 1.97 us -> none  [the longest x1 1.87 us: per_device(): frames = samples[0].reshape(local_inputs, frame_count, points)]
    squeeze x3 -> x0, local copies, waits for them, and re-layouts: 1.37 us -> none  [the longest x1 1.24 us: make_correlate(): right = jnp.concatenate([piece[0], piece[1]], axis=1)]
  transfers between devices with their start and end apart: 1 -> 0, of which waited for: 1 -> 0; matrix products, arithmetic and copies ran while one was open for 3% -> 0% of each run, Pallas kernels for 0% -> 0%
where the time goes in v2:
time: 71.4 us; the launch traced here: 71.1 us
  Pallas kernels  64.9 us (91%)
  local copies, waits for them, and re-layouts  6.28 us (9%)
    pallas_call x1, Pallas kernels, per_device(): pl.pallas_call(functools.partial(body, 1.0 / count), out_shape=jax.ShapeD...  64.9 us
    unnamed x11, local copies, waits for them, and re-layouts  6.28 us

profile of v2, /device:TPU:1, one launch (start us, length us, event | category | flops | bytes accessed | tf_op | source)
XLA Modules:
  0.0 71.1 jit_solution(16031712348799843973)
XLA Ops:
  0.0 0.0 copy-start
  0.0 1.2 %copy-done = bf16[1,4,131840]{2,1,0:T(4,128)(2,1)S(1)} copy-done((bf16[1,4,131840]{2,1,0:T(4,128)(2,1)S(1)}, bf16[1,4,131840]{2,1,0:T(4,128)(2,1)}, u32[]{:S(2)}) %copy-start) | copy-done | bytes 1054744
  1.2 0.0 copy-start.1
  1.2 1.0 %copy-done.1 = bf16[2,256,512]{2,1,0:T(8,128)(2,1)S(1)} copy-done((bf16[2,256,512]{2,1,0:T(8,128)(2,1)S(1)}, bf16[2,256,512]{2,1,0:T(8,128)(2,1)}, u32[]{:S(2)}) %copy-start.1) | copy-done | bytes 524312
  2.3 0.0 copy-start.2
  2.3 0.7 copy-done.2
  3.0 0.0 copy-start.3
  3.0 0.7 copy-done.3
  3.6 0.0 copy-start.4
  3.6 0.7 copy-done.4
  4.3 64.9 %correlator.1 = f32[1,2,256,2048]{3,2,1,0:T(8,128)S(1)} custom-call(bf16[1,4,131840]{2,1,0:T(4,128)(2,1)S(1)} %copy-done, f32[4,256]{1,0:T(4,128)S(1)} %copy-done.2, s32[1,64]{1,0:T(1,128)S(1)} %bitcast.1, s32[1,4]{1,0:T(1,128)S(1)} %copy-done.4, bf16[2,256,512]{2,1,0:T(8,128)(2,1)S(1)} %copy-done.1), custom_call_target="tpu_custom_call" | custom-call | tf_op jit(solution)/shard_map/correlator/pallas_call | solution.py:356
  69.1 2.0 %copy.7 = f32[1,2,256,2048]{3,2,1,0:T(8,128)} copy(f32[1,2,256,2048]{3,2,1,0:T(8,128)S(1)} %correlator.1) | data formatting | bytes 8388608
Async XLA Ops:
  0.0 1.2 %copy-start = (bf16[1,4,131840]{2,1,0:T(4,128)(2,1)S(1)}, bf16[1,4,131840]{2,1,0:T(4,128)(2,1)}, u32[]{:S(2)}) copy-start(bf16[1,4,131840]{2,1,0:T(4,128)(2,1)} %samples_hbm.1) | copy-start | bytes 3164164
  1.2 1.0 %copy-start.1 = (bf16[2,256,512]{2,1,0:T(8,128)(2,1)S(1)}, bf16[2,256,512]{2,1,0:T(8,128)(2,1)}, u32[]{:S(2)}) copy-start(bf16[2,256,512]{2,1,0:T(8,128)(2,1)} %constant.2.clone.twiddle_hbm) | copy-start | bytes 1572868
  2.3 0.7 copy-start.2
  3.0 0.7 copy-start.3
  3.6 0.7 copy-start.4

commit v3 on v2

v3 whole, which is shorter than its diff:
```python
import functools
import math

import jax
import jax.numpy as jnp
from jax import lax
from jax.experimental import pallas as pl
from jax.experimental.pallas import tpu as pltpu
from jax.sharding import PartitionSpec as P

MESH = pl.DeviceIdType.MESH
F32, BF16 = jnp.float32, jnp.bfloat16
NX, NY, NZ = 4, 8, 8
UNROLL = 4
CH = 4
NT = (((1,), (1,)), ((), ()))
REL = (0, -1, 1, -2, 2, -3, 3, 4)


def place():
    chan, tile, core = lax.axis_index("chan"), lax.axis_index("tile"), lax.axis_index("cores")
    return chan // (2 * NY), chan % NY, tile * 2 + (chan // NY) % 2, core


def device(x, y, z, core):
    x, y, z = x % NX, y % NY, z % NZ
    return ((x * 2 + z % 2) * NY + y, z // 2, core)


def body(
    scale, samples, small, vis,
    table, wide, spec, yr, turned, xs, held, za, zb, zx, got, left,
    ysend, yrecv, xsend, xrecv, zsend, zrecv, csend, crecv, own, y0send, y0recv, x0send, x0recv,
):
    x, y, z, k = place()
    inputs, points, count = samples.shape[1], small.shape[1], small.shape[0] - 2
    chunk_blocks, extra = 256, 2 * (count - 1)

    def wait(ref, sem):
        pltpu.make_async_copy(ref, ref, sem).wait()

    def remote(src, dst, ssem, rsem, dev):
        pltpu.make_async_remote_copy(
            src_ref=src, dst_ref=dst, send_sem=ssem, recv_sem=rsem, device_id=dev, device_id_type=MESH
        ).start()

    sib = device(x, y, z, 1 - k)
    barrier = pltpu.get_barrier_semaphore()
    partners = [device(x, y + d, z, k) for d in range(1, NY)]
    partners += [device(x + d, y, z, k) for d in range(1, NX)]
    partners += [device(x, y, z + d, k) for d in (1, 2, NZ - 1, NZ - 2)] + [sib]
    for d in partners:
        pl.semaphore_signal(barrier, inc=1, device_id=d, device_id_type=MESH)

    height, channels = table.shape[1], table.shape[1] // 2
    row = lax.broadcasted_iota(jnp.int32, (height, channels), 0)
    origin = (((row >> 1) & 3) * 2 + (row >> 6)) * NY + ((row >> 3) & 7)
    select = (origin == lax.broadcasted_iota(jnp.int32, row.shape, 1)).astype(F32).astype(BF16)
    kept = jnp.broadcast_to(small[pl.ds(count, 1), pl.ds(0, channels)], (points, channels)).astype(BF16)
    channel = lax.dot_general(select, kept, NT, preferred_element_type=F32).astype(jnp.int32)
    sample = lax.broadcasted_iota(jnp.int32, (height, points), 1)
    quarter = (lax.broadcasted_iota(jnp.int32, (height, points), 0) & 1) * (points // 4)
    turn_at = ((channel * sample + quarter + points // 2) & (points - 1)) - points // 2
    angle = turn_at.astype(F32) * (math.pi / points)
    square = angle * angle
    series = jnp.full(square.shape, 1.0 / math.factorial(13), F32)
    for order in (11, 9, 7, 5, 3, 1):
        series = (-1) ** (order // 2) / math.factorial(order) + square * series
    sine = angle * series
    whole = (1.0 - 2.0 * sine * sine) * (1.0 / math.sqrt(points))
    table[0] = whole.astype(BF16)
    table[1] = (whole - table[0].astype(F32)).astype(BF16)

    stride = 2 * inputs

    def widen(h):
        start = 0 if h == 0 else h * chunk_blocks + extra
        size = chunk_blocks + (extra if h == 0 else 0)
        unroll = 16 if size % 16 == 0 else 2

        def step(s, _):
            for u in range(unroll):
                block = start + s * unroll + u
                values = samples[0, :, pl.ds(pl.multiple_of(block * 128, 128), 128)].astype(F32)
                wide[pl.ds(pl.multiple_of(block * inputs, inputs), inputs), :] = values
            return 0

        lax.fori_loop(0, size // unroll, step, 0)

    def transform(h, i):
        halves = []
        for half in range(2):
            total = None
            for t in range(count):
                rows = wide[pl.ds((h * 128 + t) * stride + half * inputs + i, 128, stride=stride), :]
                term = small[pl.ds(t, 1), pl.ds(half * 128, 128)] * rows
                total = term if total is None else total + term
            halves.append(total)
        filtered = jnp.concatenate(halves, axis=1)
        high = filtered.astype(BF16)
        low = (filtered - high.astype(F32)).astype(BF16)
        spectrum = lax.dot_general(table[0], high, NT, preferred_element_type=F32)
        spectrum += lax.dot_general(table[0], low, NT, preferred_element_type=F32)
        spectrum += lax.dot_general(table[1], high, NT, preferred_element_type=F32)
        return spectrum * small[pl.ds(count + 1, 1), pl.ds(i, 1)]

    def spectra(h):
        widen(h)
        for m in range(inputs // 2):
            pair = [transform(h, 2 * m + i).reshape(2, NY, 8, 128) for i in range(2)]
            spec[h, :, :, m] = jnp.concatenate(pair, axis=2).astype(BF16)

    def send_y(h):
        pltpu.make_async_copy(spec.at[h, :, y], yr.at[h - 1, :, y], yrecv.at[h - 1]).start()
        for d in (4, 3, 5, 2, 6, 1, 7):
            to = (y + d) % NY
            remote(spec.at[h, :, to], yr.at[h - 1, :, y], ysend, yrecv.at[h - 1], device(x, y + d, z, k))

    def wait_y(h):
        wait(yr.at[h - 1], yrecv.at[h - 1])

    def turn(block, write):
        turned[...] = block.reshape(turned.shape).astype(F32)
        for r in range(8):
            write(r // 2, r % 2, turned[pl.ds(r, 32, stride=8), :].astype(BF16))

    def send_x(h):
        for p in range(2):

            def write(xc, q, values, p=p):
                xs[h - 2, xc, p, :, pl.ds(q * 128, 128)] = values

            turn(yr[h - 1, p], write)
        pltpu.make_async_copy(xs.at[h - 2, x], held.at[h - 2, x], xrecv.at[h - 2]).start()
        for d in (2, 1, 3):
            to = (x + d) % NX
            remote(xs.at[h - 2, to], held.at[h - 2, x], xsend, xrecv.at[h - 2], device(x + d, y, z, k))

    def slot(h, n):
        src = (z + REL[n]) % NZ
        return got.at[h, (src // 2) * 2 + k, :, src % 2]

    def forward(h, n):
        remote(slot(h, n), slot(h, n), csend, crecv.at[h, n // 5], sib)

    def spread(h, same, other, at):
        spread_odd(h, other, at)
        spread_even(h, same, at)

    def spread_odd(h, other, at):
        remote(other, at(0, 1), zsend, zrecv.at[h, 1], device(x, y, z + 1, k))
        remote(other, at(0, 2), zsend, zrecv.at[h, 2], device(x, y, z - 1, k))

    def spread_even(h, same, at):
        remote(same, at(0, 3), zsend, zrecv.at[h, 3], device(x, y, z + 2, k))
        remote(same, at(0, 4), zsend, zrecv.at[h, 4], device(x, y, z - 2, k))
        pltpu.make_async_copy(same, at(0, 0), own.at[h]).start()

    def relay(h, at):
        relay_odd(h, at)
        relay_even(h, at)

    def relay_odd(h, at):
        wait(at(1, 1), zrecv.at[h, 1])
        remote(at(1, 1), at(1, 5), zsend, zrecv.at[h, 5], device(x, y, z + 2, k))
        wait(at(2, 2), zrecv.at[h, 2])
        remote(at(2, 2), at(2, 6), zsend, zrecv.at[h, 6], device(x, y, z - 2, k))

    def relay_even(h, at):
        sign = (h + k) % 2
        wait(at(3, 3), zrecv.at[h, 3])
        wait(at(4, 4), zrecv.at[h, 4])
        remote(at(3 + sign, 3 + sign), at(3 + sign, 7), zsend, zrecv.at[h, 7], device(x, y, z + 2 - 4 * sign, k))

    def at_early(h):
        def at(_, n):
            return za.at[h, n]

        return at

    def at_slot(h):
        def at(n, _):
            if isinstance(n, int):
                return slot(h, n)
            src = (z - 2 + 4 * (n - 3)) % NZ
            return got.at[h, (src // 2) * 2 + k, :, src % 2]

        return at

    def spread_early(h):
        spread(h, yr.at[0, z % 2], yr.at[0, 1 - z % 2], at_early(h))

    def relay_early(h):
        relay(h, at_early(h))
        wait(za.at[h, 0], own.at[h])

    def finish_early(h):
        for n in range(5, 8):
            wait(za.at[h, n], zrecv.at[h, n])

    def send_z(h):
        wait(held.at[h - 2], xrecv.at[h - 2])
        same, other = held.at[h - 2, :, z % 2], held.at[h - 2, :, 1 - z % 2]
        spread(h, same, other, at_slot(h))
        remote(same, slot(h, 0), csend, crecv.at[h, 0], sib)

    def relay_z(h):
        relay(h, at_slot(h))
        for n in range(1, 5):
            forward(h, n)

    def finish_z(h):
        for n in range(5, 8):
            wait(slot(h, n), zrecv.at[h, n])
            forward(h, n)

    groups = ((0, 5), (5, 3))

    def send_y0(g):
        begin, size = groups[g]
        mine = pl.ds(begin, size)
        pltpu.make_async_copy(za.at[0, mine, y], zb.at[y, mine], y0recv.at[g]).start()
        for d in (4, 3, 5, 2, 6, 1, 7):
            to = (y + d) % NY
            remote(za.at[0, mine, to], zb.at[y, mine], y0send, y0recv.at[g], device(x, y + d, z, k))

    def send_x_late(h, g):
        begin, size = groups[g]
        if h == 0:
            wait(zb.at[:, pl.ds(begin, size)], y0recv.at[g])
        for n in range(begin, begin + size):

            def write(xc, q, values, n=n):
                zx[h, xc, n, :, pl.ds(q * 128, 128)] = values

            turn(za[1, n] if h else zb[:, n], write)
            src = (z + REL[n]) % NZ
            dst = got.at[h, (src // 2) * 2 + k, x, src % 2]
            pltpu.make_async_copy(zx.at[h, x, n], dst, x0recv.at[h, n]).start()
            for d in (2, 1, 3):
                remote(zx.at[h, (x + d) % NX, n], dst, x0send, x0recv.at[h, n], device(x + d, y, z, k))

    def finish_x_late(h, g):
        begin, size = groups[g]
        for n in range(begin, begin + size):
            wait(slot(h, n), x0recv.at[h, n])
            forward(h, n)

    rows = vis.shape[2]

    def lay(h, b):
        return got[h, b].reshape(rows, 256)

    def lay_left(h):
        block = lay(h, (z // 2) * 2 + k)
        left[h, pl.ds(0, rows)] = block
        left[h, pl.ds(rows, rows), pl.ds(0, 128)] = block[:, 128:]
        left[h, pl.ds(rows, rows), pl.ds(128, 128)] = -block[:, :128]

    def product(h, b):
        return lax.dot_general(left[h], lay(h, b), NT, preferred_element_type=F32).reshape(2, rows, rows)

    def columns(b):
        return pl.ds(pl.multiple_of(b * rows, rows), rows)

    def wait_sibling(h, g):
        begin, size = groups[g]
        wait(got.at[h, pl.ds(begin, size), :, 0], crecv.at[h, g])

    def correlate(h, start=False):
        if h > 1:
            wait(slot(h, 0), own.at[h])
        wait_sibling(h, 0)
        wait_sibling(h, 1)
        lay_left(h)

        def step(b, _):
            vis[0, :, :, columns(b)] = product(h, b) if start else vis[0, :, :, columns(b)] + product(h, b)
            return 0

        lax.fori_loop(0, 8, step, 0, unroll=UNROLL)

    def multiply(h, b):
        vis[0, :, :, columns(b)] = (vis[0, :, :, columns(b)] + product(h, b)) * scale

    def correlate_last(h):
        side = 2 * (z % 2) - 1
        tiles = ((z // 2) % 4, (z // 2 + side) % 4, (z // 2 - side) % 4, (z // 2 + 2) % 4)
        wait(slot(h, 0), own.at[h])
        lay_left(h)
        for t in tiles:
            multiply(h, t * 2 + k)
        wait_sibling(h, 0)
        for t in tiles[:2]:
            multiply(h, t * 2 + 1 - k)
        wait_sibling(h, 1)
        for t in tiles[2:]:
            multiply(h, t * 2 + 1 - k)

    spectra(0)
    pl.semaphore_wait(barrier, len(partners))
    spread_odd(0, spec.at[0, 1 - z % 2], at_early(0))
    spectra(1)
    spread_even(0, spec.at[0, z % 2], at_early(0))
    send_y(1)
    spectra(2)
    send_y(2)
    relay_odd(0, at_early(0))
    spectra(3)
    send_y(3)
    relay_even(0, at_early(0))
    wait(za.at[0, 0], own.at[0])
    wait_y(1)
    spread_early(1)
    wait_y(2)
    send_x(2)
    send_y0(0)
    wait_y(3)
    send_x(3)
    send_z(2)
    finish_early(0)
    send_y0(1)
    relay_early(1)
    send_x_late(1, 0)
    send_z(3)
    relay_z(2)
    finish_early(1)
    send_x_late(1, 1)
    send_x_late(0, 0)
    relay_z(3)
    send_x_late(0, 1)
    finish_x_late(1, 0)
    finish_x_late(1, 1)
    finish_x_late(0, 0)
    correlate(1, start=True)
    finish_x_late(0, 1)
    finish_z(2)
    correlate(0)
    finish_z(3)
    correlate(2)
    correlate_last(3)

    wait(got.at[:, pl.ds(0, 4)], csend)
    wait(got.at[:, pl.ds(0, 7), :, 0], zsend)
    wait(spec.at[pl.ds(0, CH - 1), :, pl.ds(0, NY - 1)], ysend)
    wait(xs.at[:, pl.ds(0, NX - 1)], xsend)
    wait(za.at[0, pl.ds(0, NY - 1)], y0send)
    wait(zx.at[:, pl.ds(0, NX - 1)], x0send)


def per_device(samples, filter_taps, kept_channels, input_flags):
    count, points = filter_taps.shape
    inputs, length = samples.shape[1:]
    spectra = length // points - count + 1
    channels = kept_channels.shape[0]
    vmem = pl.BlockSpec(memory_space=pltpu.VMEM)
    dma = pltpu.SemaphoreType.DMA
    rows = 256
    late = CH - 1
    def lengthen(values):
        return jnp.pad(values, ((0, 0), (0, points - values.shape[1]))).astype(F32)

    small = jnp.concatenate([filter_taps, lengthen(kept_channels[None]), lengthen(input_flags)])

    return pl.pallas_call(
        functools.partial(body, 1.0 / spectra),
        out_shape=jax.ShapeDtypeStruct((1, 2, rows, 8 * rows), F32),
        in_specs=[vmem] * 2,
        out_specs=vmem,
        scratch_shapes=[
            pltpu.VMEM((2, 2 * channels, points), BF16),
            pltpu.VMEM((length // 128 * inputs, 128), F32),
            pltpu.VMEM((CH, 2, NY, 2, 16, 128), BF16),
            pltpu.VMEM((late, 2, NY, 2, 16, 128), BF16),
            pltpu.VMEM((NY * inputs * 8, 128), F32),
            pltpu.VMEM((2, NX, 2, 32, 256), BF16),
            pltpu.VMEM((2, NX, 2, 32, 256), BF16),
            pltpu.VMEM((2, 8, NY, 2, 16, 128), BF16),
            pltpu.VMEM((NY, 8, 2, 16, 128), BF16),
            pltpu.VMEM((2, NX, 8, 32, 256), BF16),
            pltpu.VMEM((CH, 8, NX, 2, 32, 256), BF16),
            pltpu.VMEM((CH, 2 * rows, 256), BF16),
            dma,
            dma((late,)),
            dma,
            dma((2,)),
            dma,
            dma((CH, 8)),
            dma,
            dma((CH, 2)),
            dma((CH,)),
            dma,
            dma((2,)),
            dma,
            dma((2, 8)),
        ],
        compiler_params=pltpu.CompilerParams(
            collective_id=0, has_side_effects=True, vmem_limit_bytes=40 << 20
        ),
        name="correlator",
    )(samples, small)


def solution(mesh):
    in_specs = (P(("tile", "cores"), "chan", None), P(), P(), P(("tile", "cores"), "chan"))
    out_specs = P("chan", None, ("tile", "cores"), None)
    return jax.shard_map(
        per_device, mesh=mesh, in_specs=in_specs, out_specs=out_specs, check_vma=False
    )
```

time: 71.4 us -> 60 us (0.84)
  Pallas kernels: 64.9 us -> 55.2 us
  local copies, waits for them, and re-layouts: 6.28 us -> 3.24 us
  other arithmetic: 0 us -> 1.37 us
    pallas_call x1, Pallas kernels: 64.9 us -> 55.2 us  [per_device(): pl.pallas_call(functools.partial(body, 1.0 / spectra), out_shape=jax.Shap...]
    unnamed x11 -> x3, local copies, waits for them, and re-layouts: 6.28 us -> 3.24 us
where the time goes in v3:
time: 60 us; the launch traced here: 59.8 us
  Pallas kernels  55.2 us (92%)
  local copies, waits for them, and re-layouts  3.24 us (5%)
  other arithmetic  1.37 us (2%)
    pallas_call x1, Pallas kernels, per_device(): pl.pallas_call(functools.partial(body, 1.0 / spectra), out_shape=jax.Shap...  55.2 us
    unnamed x3, local copies, waits for them, and re-layouts  3.24 us

profile of v3, /device:TPU:1, one launch (start us, length us, event | category | flops | bytes accessed | tf_op | source)
XLA Modules:
  0.0 59.8 jit_solution(17694378649506298318)
XLA Ops:
  0.0 0.7 %pad_convert_fusion = (f32[1,256]{1,0:T(1,128)S(1)}, f32[1,256]{1,0:T(1,128)S(1)}) fusion(s32[1,4]{1,0:T(1,128)} %param.7, s32[1,64]{1,0:T(1,128)} %bitcast.1), kind=kLoop, calls=%fused_computation.1 | loop fusion | flops 512 | bytes 2320 | tf_op jit(solution)/shard_map/convert_element_type | solution.py:361
  0.7 0.7 %pad_maximum_fusion.small = f32[6,256]{1,0:T(8,128)S(1)} fusion(f32[1,256]{1,0:T(1,128)S(1)} %get-tuple-element.5, f32[1,256]{1,0:T(1,128)S(1)} %get-tuple-element.6, f32[4,256]{1,0:T(4,128)} %param.5), kind=kLoop, calls=%fused_computation | loop fusion | flops 3072 | bytes 12288 | tf_op jit(solution)/shard_map/concatenate | solution.py:363
  1.4 0.0 copy-start
  1.4 1.2 %copy-done = bf16[1,4,131840]{2,1,0:T(4,128)(2,1)S(1)} copy-done((bf16[1,4,131840]{2,1,0:T(4,128)(2,1)S(1)}, bf16[1,4,131840]{2,1,0:T(4,128)(2,1)}, u32[]{:S(2)}) %copy-start) | copy-done | bytes 1054744
  2.6 55.2 %correlator.1 = f32[1,2,256,2048]{3,2,1,0:T(8,128)S(1)} custom-call(bf16[1,4,131840]{2,1,0:T(4,128)(2,1)S(1)} %copy-done, f32[6,256]{1,0:T(8,128)S(1)} %pad_maximum_fusion.small), custom_call_target="tpu_custom_call" | custom-call | tf_op jit(solution)/shard_map/correlator/pallas_call | solution.py:365
  57.8 2.0 %copy.6 = f32[1,2,256,2048]{3,2,1,0:T(8,128)} copy(f32[1,2,256,2048]{3,2,1,0:T(8,128)S(1)} %correlator.1) | data formatting | bytes 8388608
Async XLA Ops:
  1.4 1.2 %copy-start = (bf16[1,4,131840]{2,1,0:T(4,128)(2,1)S(1)}, bf16[1,4,131840]{2,1,0:T(4,128)(2,1)}, u32[]{:S(2)}) copy-start(bf16[1,4,131840]{2,1,0:T(4,128)(2,1)} %samples.1) | copy-start | bytes 3164164

commit v4 on v3

--- a/solution.py
+++ b/solution.py
@@ -28,12 +28,12 @@
 
 
 def body(
-    scale, samples, small, vis,
-    table, wide, spec, yr, turned, xs, held, za, zb, zx, got, left,
+    scale, samples_hbm, taps_hbm, kept_hbm, flags_hbm, vis,
+    samples, taps, kept, flags, load, table, wide, spec, yr, turned, xs, held, za, zb, zx, got, left,
     ysend, yrecv, xsend, xrecv, zsend, zrecv, csend, crecv, own, y0send, y0recv, x0send, x0recv,
 ):
     x, y, z, k = place()
-    inputs, points, count = samples.shape[1], small.shape[1], small.shape[0] - 2
+    inputs, (count, points) = samples.shape[1], taps.shape
     chunk_blocks, extra = 256, 2 * (count - 1)
 
     def wait(ref, sem):
@@ -43,6 +43,21 @@
         pltpu.make_async_remote_copy(
             src_ref=src, dst_ref=dst, send_sem=ssem, recv_sem=rsem, device_id=dev, device_id_type=MESH
         ).start()
+
+    def piece(h):
+        start = 0 if h == 0 else h * chunk_blocks + extra
+        return start, chunk_blocks + (extra if h == 0 else 0)
+
+    loads = [
+        pltpu.make_async_copy(src, dst, load.at[CH + n])
+        for n, (src, dst) in enumerate(((kept_hbm, kept), (taps_hbm, taps), (flags_hbm, flags)))
+    ]
+    for h in range(CH):
+        start, size = piece(h)
+        where = (slice(None), slice(None), pl.ds(start * 128, size * 128))
+        loads.append(pltpu.make_async_copy(samples_hbm.at[where], samples.at[where], load.at[h]))
+    for copy in loads:
+        copy.start()
 
     sib = device(x, y, z, 1 - k)
     barrier = pltpu.get_barrier_semaphore()
@@ -52,12 +67,15 @@
     for d in partners:
         pl.semaphore_signal(barrier, inc=1, device_id=d, device_id_type=MESH)
 
+    for copy in loads[:3]:
+        copy.wait()
+
     height, channels = table.shape[1], table.shape[1] // 2
     row = lax.broadcasted_iota(jnp.int32, (height, channels), 0)
     origin = (((row >> 1) & 3) * 2 + (row >> 6)) * NY + ((row >> 3) & 7)
     select = (origin == lax.broadcasted_iota(jnp.int32, row.shape, 1)).astype(F32).astype(BF16)
-    kept = jnp.broadcast_to(small[pl.ds(count, 1), pl.ds(0, channels)], (points, channels)).astype(BF16)
-    channel = lax.dot_general(select, kept, NT, preferred_element_type=F32).astype(jnp.int32)
+    spread_kept = jnp.broadcast_to(kept[...].astype(F32), (points, channels)).astype(BF16)
+    channel = lax.dot_general(select, spread_kept, NT, preferred_element_type=F32).astype(jnp.int32)
     sample = lax.broadcasted_iota(jnp.int32, (height, points), 1)
     quarter = (lax.broadcasted_iota(jnp.int32, (height, points), 0) & 1) * (points // 4)
     turn_at = ((channel * sample + quarter + points // 2) & (points - 1)) - points // 2
@@ -74,8 +92,8 @@
     stride = 2 * inputs
 
     def widen(h):
-        start = 0 if h == 0 else h * chunk_blocks + extra
-        size = chunk_blocks + (extra if h == 0 else 0)
+        loads[3 + h].wait()
+        start, size = piece(h)
         unroll = 16 if size % 16 == 0 else 2
 
         def step(s, _):
@@ -93,7 +111,7 @@
             total = None
             for t in range(count):
                 rows = wide[pl.ds((h * 128 + t) * stride + half * inputs + i, 128, stride=stride), :]
-                term = small[pl.ds(t, 1), pl.ds(half * 128, 128)] * rows
+                term = taps[pl.ds(t, 1), pl.ds(half * 128, 128)] * rows
                 total = term if total is None else total + term
             halves.append(total)
         filtered = jnp.concatenate(halves, axis=1)
@@ -102,7 +120,7 @@
         spectrum = lax.dot_general(table[0], high, NT, preferred_element_type=F32)
         spectrum += lax.dot_general(table[0], low, NT, preferred_element_type=F32)
         spectrum += lax.dot_general(table[1], high, NT, preferred_element_type=F32)
-        return spectrum * small[pl.ds(count + 1, 1), pl.ds(i, 1)]
+        return spectrum * flags[pl.ds(0, 1), pl.ds(i, 1)].astype(F32)
 
     def spectra(h):
         widen(h)
@@ -280,22 +298,23 @@
 
         lax.fori_loop(0, 8, step, 0, unroll=UNROLL)
 
-    def multiply(h, b):
-        vis[0, :, :, columns(b)] = (vis[0, :, :, columns(b)] + product(h, b)) * scale
-
-    def correlate_last(h):
-        side = 2 * (z % 2) - 1
-        tiles = ((z // 2) % 4, (z // 2 + side) % 4, (z // 2 - side) % 4, (z // 2 + 2) % 4)
-        wait(slot(h, 0), own.at[h])
-        lay_left(h)
-        for t in tiles:
-            multiply(h, t * 2 + k)
-        wait_sibling(h, 0)
-        for t in tiles[:2]:
-            multiply(h, t * 2 + 1 - k)
-        wait_sibling(h, 1)
-        for t in tiles[2:]:
-            multiply(h, t * 2 + 1 - k)
+    def multiply(chunks, b):
+        total = vis[0, :, :, columns(b)]
+        for h in chunks:
+            total = total + product(h, b)
+        vis[0, :, :, columns(b)] = total * scale
+
+    def correlate_last(*chunks):
+        wait(slot(CH - 1, 0), own.at[CH - 1])
+        for h in chunks:
+            lay_left(h)
+        for t in range(4):
+            multiply(chunks, t * 2 + k)
+        for h in chunks:
+            wait_sibling(h, 0)
+            wait_sibling(h, 1)
+        for t in range(4):
+            multiply(chunks, t * 2 + 1 - k)
 
     spectra(0)
     pl.semaphore_wait(barrier, len(partners))
@@ -331,14 +350,13 @@
     send_x_late(0, 1)
     finish_x_late(1, 0)
     finish_x_late(1, 1)
+    finish_z(2)
     finish_x_late(0, 0)
     correlate(1, start=True)
+    correlate(2)
     finish_x_late(0, 1)
-    finish_z(2)
-    correlate(0)
     finish_z(3)
-    correlate(2)
-    correlate_last(3)
+    correlate_last(0, 3)
 
     wait(got.at[:, pl.ds(0, 4)], csend)
     wait(got.at[:, pl.ds(0, 7), :, 0], zsend)
@@ -357,17 +375,16 @@
     dma = pltpu.SemaphoreType.DMA
     rows = 256
     late = CH - 1
-    def lengthen(values):
-        return jnp.pad(values, ((0, 0), (0, points - values.shape[1]))).astype(F32)
-
-    small = jnp.concatenate([filter_taps, lengthen(kept_channels[None]), lengthen(input_flags)])
+    operands = (samples, filter_taps, kept_channels.reshape(1, channels), input_flags)
 
     return pl.pallas_call(
         functools.partial(body, 1.0 / spectra),
         out_shape=jax.ShapeDtypeStruct((1, 2, rows, 8 * rows), F32),
-        in_specs=[vmem] * 2,
+        in_specs=[pl.BlockSpec(memory_space=pl.ANY)] * 4,
         out_specs=vmem,
         scratch_shapes=[
+            *(pltpu.VMEM(a.shape, a.dtype) for a in operands),
+            dma((CH + 3,)),
             pltpu.VMEM((2, 2 * channels, points), BF16),
             pltpu.VMEM((length // 128 * inputs, 128), F32),
             pltpu.VMEM((CH, 2, NY, 2, 16, 128), BF16),
@@ -398,7 +415,7 @@
             collective_id=0, has_side_effects=True, vmem_limit_bytes=40 << 20
         ),
         name="correlator",
-    )(samples, small)
+    )(*(pltpu.with_memory_space_constraint(a, pltpu.HBM) for a in operands))
 
 
 def solution(mesh):

time: 60 us -> 57.5 us (0.958)
  the two profiles are of different devices: /device:TPU:1 before, /device:TPU:7 now
where the time goes in v4:
time: 57.5 us; the launch traced here: 57.4 us
  Pallas kernels  55.4 us (96%)
  local copies, waits for them, and re-layouts  2.02 us (4%)
    pallas_call x1, Pallas kernels, per_device(): pl.pallas_call(functools.partial(body, 1.0 / spectra), out_shape=jax.Shap...  55.4 us
    unnamed x1, local copies, waits for them, and re-layouts  2.02 us

profile of v4, /device:TPU:7, one launch (start us, length us, event | category | flops | bytes accessed | tf_op | source)
XLA Modules:
  0.0 57.4 jit_solution(9041577862482705354)
XLA Ops:
  0.0 55.4 %correlator.1 = f32[1,2,256,2048]{3,2,1,0:T(8,128)S(1)} custom-call(bf16[1,4,131840]{2,1,0:T(4,128)(2,1)} %samples_hbm.1, f32[4,256]{1,0:T(4,128)} %taps_hbm.1, s32[1,64]{1,0:T(1,128)} %bitcast.1, s32[1,4]{1,0:T(1,128)} %flags_hbm.1), custom_call_target="tpu_custom_call" | custom-call | tf_op jit(solution)/shard_map/correlator/pallas_call | solution.py:380
  55.4 2.0 %copy.6 = f32[1,2,256,2048]{3,2,1,0:T(8,128)} copy(f32[1,2,256,2048]{3,2,1,0:T(8,128)S(1)} %correlator.1) | data formatting | bytes 8388608

commit v5 on v4

--- a/solution.py
+++ b/solution.py
@@ -305,15 +305,21 @@
         vis[0, :, :, columns(b)] = total * scale
 
     def correlate_last(*chunks):
+        side = 2 * (z % 2) - 1
+        tiles = (z // 2, (z // 2 + side) % 4, (z // 2 - side) % 4, (z // 2 + 2) % 4)
         wait(slot(CH - 1, 0), own.at[CH - 1])
         for h in chunks:
             lay_left(h)
-        for t in range(4):
+        for t in tiles:
             multiply(chunks, t * 2 + k)
-        for h in chunks:
+        for h in chunks[:-1]:
             wait_sibling(h, 0)
             wait_sibling(h, 1)
-        for t in range(4):
+        wait_sibling(chunks[-1], 0)
+        for t in tiles[:2]:
+            multiply(chunks, t * 2 + 1 - k)
+        wait_sibling(chunks[-1], 1)
+        for t in tiles[2:]:
             multiply(chunks, t * 2 + 1 - k)
 
     spectra(0)
@@ -340,8 +346,8 @@
     finish_early(0)
     send_y0(1)
     relay_early(1)
+    send_z(3)
     send_x_late(1, 0)
-    send_z(3)
     relay_z(2)
     finish_early(1)
     send_x_late(1, 1)
@@ -353,9 +359,9 @@
     finish_z(2)
     finish_x_late(0, 0)
     correlate(1, start=True)
-    correlate(2)
     finish_x_late(0, 1)
     finish_z(3)
+    correlate(2)
     correlate_last(0, 3)
 
     wait(got.at[:, pl.ds(0, 4)], csend)

time: 57.5 us -> 56.8 us (0.988)
  the two profiles are of different devices: /device:TPU:7 before, /device:TPU:1 now
where the time goes in v5:
time: 56.8 us; the launch traced here: 55.9 us
  Pallas kernels  53.9 us (95%)
  local copies, waits for them, and re-layouts  2.02 us (4%)
    pallas_call x1, Pallas kernels, per_device(): pl.pallas_call(functools.partial(body, 1.0 / spectra), out_shape=jax.Shap...  53.9 us
    unnamed x1, local copies, waits for them, and re-layouts  2.02 us

profile of v5, /device:TPU:1, one launch (start us, length us, event | category | flops | bytes accessed | tf_op | source)
XLA Modules:
  0.0 55.9 jit_solution(2034489016290307638)
XLA Ops:
  0.0 53.9 %correlator.1 = f32[1,2,256,2048]{3,2,1,0:T(8,128)S(1)} custom-call(bf16[1,4,131840]{2,1,0:T(4,128)(2,1)} %samples_hbm.1, f32[4,256]{1,0:T(4,128)} %taps_hbm.1, s32[1,64]{1,0:T(1,128)} %bitcast.1, s32[1,4]{1,0:T(1,128)} %flags_hbm.1), custom_call_target="tpu_custom_call" | custom-call | tf_op jit(solution)/shard_map/correlator/pallas_call | solution.py:386
  53.9 2.0 %copy.6 = f32[1,2,256,2048]{3,2,1,0:T(8,128)} copy(f32[1,2,256,2048]{3,2,1,0:T(8,128)S(1)} %correlator.1) | data formatting | bytes 8388608
